TPU v7x, 32 devices: a whole 2x2x4 slice. The times are simulated.
32 devices in a mesh: grp: 4 (over x, core), shard: 8 (over z, y).
Axes of the slice: x: 2, y: 2, z: 4, core: 2. Of those that a mesh axis runs over, the one named last changes fastest.
Arguments:
- cand_table: bfloat16 [2048, 512], P('grp'), may hold values from -6 to 6
- inverse: int32 [8192], P(('grp', 'shard')), may hold values from 0 to 2047
- cache_keys: bfloat16 [65536, 512], P(('grp', 'shard')), may hold values from -6 to 6
- cache_values: bfloat16 [65536, 512], P(('grp', 'shard')), may hold values from -6 to 6
- block_dest: int32 [512, 1], P(('grp', 'shard')), may hold values from 0 to 7; in each aligned block of 16 rows (0 to 15, 16 to 31, ...) at most 2 rows name the same one
- w_in: bfloat16 [512, 1024], replicated, may hold values from -0.25 to 0.25
- w_out: bfloat16 [512, 512], replicated, may hold values from -0.25 to 0.25
Outputs:
- scored: bfloat16 [8192, 512], P(('grp', 'shard'))
Inputs may be any that keep to these rules, and one draw needn't show every extreme that they name: `block_dest`: among the 16 blocks held by one device, at most 2 name the same scorer.
All inputs are finite; a program needn't handle non-finite values.
Results may differ from a plain program's by a relative error of at most 0.0082.
Values may be sent and summed in bfloat16 or wider, within the bound.
A program may use at most 128 MiB of HBM per device.

v0:
```python
import math

import jax
import jax.numpy as jnp
from jax import lax
from jax.sharding import PartitionSpec as P

H = 8
BLK = 128


def layer_norm(inputs):
    center = inputs - jnp.mean(inputs, axis=-1, keepdims=True)
    spread = jnp.mean(center * center, axis=-1, keepdims=True)
    return center * lax.rsqrt(spread + 1e-05)


def attend(queries, key_rows, value_rows, score_scale):
    scores = jnp.einsum(
        "...chd,...khd->...hck", queries, key_rows, preferred_element_type=jnp.float32
    )
    weight_low = jax.nn.silu(score_scale * scores).astype(jnp.bfloat16)
    return jnp.einsum(
        "...hck,...khd->...chd", weight_low, value_rows, preferred_element_type=jnp.float32
    )


def on_device(cand_table, inverse, cache_keys, cache_values, block_dest, w_in, w_out):
    model_width = w_out.shape[0]
    head_count = H
    head_size = model_width // head_count
    score_scale = 1.0 / math.sqrt(head_size)
    cand_rows = inverse.shape[0]
    peer_count = lax.axis_size("shard")
    panel_piece = lax.all_gather(cand_table, "grp", axis=0, tiled=True)
    one_hot = (
        inverse[:, None] == jnp.arange(panel_piece.shape[0], dtype=jnp.int32)[None, :]
    ).astype(jnp.bfloat16)
    embedded = jnp.dot(one_hot, panel_piece, preferred_element_type=jnp.float32).astype(
        jnp.bfloat16
    )
    normed = layer_norm(embedded.astype(jnp.float32)).astype(jnp.bfloat16)
    projected = jax.nn.silu(jnp.dot(normed, w_in, preferred_element_type=jnp.float32))
    gate_u = projected[:, :model_width].astype(jnp.bfloat16)
    query_flat = projected[:, model_width:].astype(jnp.bfloat16)
    queries = query_flat.reshape(cand_rows, head_count, head_size)
    destination = block_dest[:, 0]
    block_count = destination.shape[0]
    most_each = max(2, block_count // peer_count)
    block_index = jnp.arange(block_count, dtype=jnp.int32)
    same_earlier = (destination[:, None] == destination[None, :]) & (
        block_index[None, :] < block_index[:, None]
    )
    bucket_rank = jnp.sum(same_earlier.astype(jnp.int32), axis=1)
    target_slot = destination * most_each + bucket_rank
    slot_ids = jnp.arange(peer_count * most_each, dtype=jnp.int32)
    slot_match = target_slot[None, :] == slot_ids[:, None]
    filled = jnp.any(slot_match, axis=1).astype(jnp.int32)
    source_block = jnp.sum(jnp.where(slot_match, block_index[None, :], 0), axis=1) + block_count * (
        1 - filled
    )
    zero_block = jnp.zeros((1, BLK, model_width), jnp.bfloat16)
    padded_keys = jnp.concatenate(
        [cache_keys.reshape(block_count, BLK, model_width), zero_block], axis=0
    )
    padded_values = jnp.concatenate(
        [cache_values.reshape(block_count, BLK, model_width), zero_block], axis=0
    )
    send_keys = padded_keys[source_block].reshape(peer_count, most_each * BLK, model_width)
    send_values = padded_values[source_block].reshape(peer_count, most_each * BLK, model_width)
    got_keys, got_values = (
        lax.all_to_all(send_keys, "shard", split_axis=0, concat_axis=0, tiled=True),
        lax.all_to_all(send_values, "shard", split_axis=0, concat_axis=0, tiled=True),
    )
    key_count = got_keys.shape[0] * got_keys.shape[1]
    all_keys = got_keys.reshape(key_count, head_count, head_size)
    all_values = got_values.reshape(key_count, head_count, head_size)
    span_rows = most_each * BLK * math.gcd(peer_count, 4)

    def add_span(turn_index, running):
        first_row = turn_index * span_rows
        key_rows = lax.dynamic_slice_in_dim(all_keys, first_row, span_rows, 0)
        value_rows = lax.dynamic_slice_in_dim(all_values, first_row, span_rows, 0)
        return running + attend(queries, key_rows, value_rows, score_scale)

    start_sums = jnp.zeros((cand_rows, head_count, head_size), jnp.float32)
    attended = lax.fori_loop(0, key_count // span_rows, add_span, start_sums).reshape(
        cand_rows, model_width
    )
    gated_rows = (layer_norm(attended) * gate_u.astype(jnp.float32)).astype(jnp.bfloat16)
    return jnp.dot(gated_rows, w_out, preferred_element_type=jnp.float32).astype(jnp.bfloat16)


def solution(mesh):
    in_specs = (
        P("grp", None),
        P(("grp", "shard")),
        P(("grp", "shard"), None),
        P(("grp", "shard"), None),
        P(("grp", "shard"), None),
        P(),
        P(),
    )
    out_specs = P(("grp", "shard"), None)
    return jax.shard_map(
        on_device, mesh=mesh, in_specs=in_specs, out_specs=out_specs, check_vma=False
    )
```

profile of v0, /device:TPU:0, one launch (start us, length us, event | category | flops | bytes accessed | tf_op | source)
XLA Modules:
  0.0 149.7 jit_solution(323340538564882216)
XLA Ops:
  6.5 0.9 convert_reduce_fusion
  7.5 0.7 multiply_add_fusion
  8.1 0.1 fusion.31
  8.3 0.1 select_reduce_fusion
  8.4 1.9 %concatenate.6 = bf16[17,128,512]{2,1,0:T(8,128)(2,1)S(1)} pad(bf16[16,128,512]{2,1,0:T(8,128)(2,1)} %bitcast.51, bf16[]{:T(256)} %constant.61.clone.1), padding=0_1x0_0x0_0 | pad | bytes 4325378 | tf_op jit(solution)/shard_map/concatenate | solution.py:66
  10.3 2.0 %gather_fusion = bf16[16,128,512]{2,1,0:T(8,128)(2,1)} fusion(bf16[17,128,512]{2,1,0:T(8,128)(2,1)S(1)} %concatenate.6, s32[1024]{0:T(1024)S(1)} %pad_clamp_fusion), kind=kCustom, calls=%fused_computation | custom fusion | bytes 4194368 | tf_op jit(solution)/shard_map/gather | solution.py:70
  12.3 3.9 %copy.29 = bf16[8,256,512]{1,2,0:T(8,128)(2,1)} copy(bf16[8,256,512]{2,1,0:T(8,128)(2,1)} %bitcast.49) | data formatting | bytes 4194304 | tf_op jit(solution)/shard_map/reshape | solution.py:70
  16.2 7.3 %all-to-all-start = ((bf16[8,256,512]{1,2,0:T(8,128)(2,1)}), bf16[8,256,512]{1,2,0:T(8,128)(2,1)}, u32[]{:S(2)}, u32[]{:S(2)}) async-start(bf16[8,256,512]{1,2,0:T(8,128)(2,1)} %copy.29), calls=%async_computation | async-start | bytes 4194304 | tf_op jit(solution)/shard_map/all_to_all | solution.py:73
  23.5 0.7 all-gather.2.cloned.1.call-update
  24.2 1.9 %concatenate.7 = bf16[17,128,512]{2,1,0:T(8,128)(2,1)S(1)} pad(bf16[16,128,512]{2,1,0:T(8,128)(2,1)} %bitcast.52, bf16[]{:T(256)} %constant.61.clone.1), padding=0_1x0_0x0_0 | pad | bytes 4325378 | tf_op jit(solution)/shard_map/concatenate | solution.py:63
  26.1 2.1 %gather_fusion.1 = bf16[16,128,512]{2,1,0:T(8,128)(2,1)} fusion(bf16[17,128,512]{2,1,0:T(8,128)(2,1)S(1)} %concatenate.7, s32[1024]{0:T(1024)S(1)} %pad_clamp_fusion), kind=kCustom, calls=%fused_computation.1 | custom fusion | bytes 4194368 | tf_op jit(solution)/shard_map/gather | solution.py:69
  28.2 3.9 %copy.31 = bf16[8,256,512]{1,2,0:T(8,128)(2,1)} copy(bf16[8,256,512]{2,1,0:T(8,128)(2,1)} %bitcast.48) | data formatting | bytes 4194304 | tf_op jit(solution)/shard_map/reshape | solution.py:69
  32.1 39.7 %all-to-all-done = bf16[8,256,512]{1,2,0:T(8,128)(2,1)} async-done(((bf16[8,256,512]{1,2,0:T(8,128)(2,1)}), bf16[8,256,512]{1,2,0:T(8,128)(2,1)}, u32[]{:S(2)}, u32[]{:S(2)}) %all-to-all-start) | async-done | bytes 2097184 | tf_op jit(solution)/shard_map/all_to_all | solution.py:73
  71.8 3.6 %all-to-all-start.1 = ((bf16[8,256,512]{1,2,0:T(8,128)(2,1)}), bf16[8,256,512]{1,2,0:T(8,128)(2,1)S(1)}, u32[]{:S(2)}, u32[]{:S(2)}) async-start(bf16[8,256,512]{1,2,0:T(8,128)(2,1)} %copy.31), calls=%async_computation.1 | async-start | bytes 4194304 | tf_op jit(solution)/shard_map/all_to_all | solution.py:72
  75.5 2.4 %fusion.34 = (f32[256]{0:T(256)S(1)}, f32[256,512]{1,0:T(8,128)S(1)}) fusion(bf16[2048,512]{1,0:T(8,128)(2,1)} %all-gather.2.cloned.1.call-done, s32[256]{0:T(256)S(1)} %copy-done.6), kind=kOutput, calls=%fused_computation.48 | convolution fusion | flops 537788160 | bytes 2623488 | tf_op jit(solution)/shard_map/dot_general | solution.py:39
  77.9 0.2 multiply_reduce_fusion.1
  78.2 0.6 multiply_convert_fusion
  78.8 0.8 copy-done.3
  79.6 0.8 copy.33
  80.4 4.1 %copy.30 = bf16[8,256,512]{1,0,2:T(8,128)(2,1)} copy(bf16[8,256,512]{1,2,0:T(8,128)(2,1)} %all-to-all-done) | data formatting | bytes 4194304 | tf_op jit(solution)/shard_map/all_to_all | solution.py:73
  84.5 4.2 %reshape.100 = bf16[2048,8,64]{0,2,1:T(8,128)(2,1)} reshape(bf16[8,256,512]{1,0,2:T(8,128)(2,1)} %copy.30) | data formatting | bytes 4194304 | tf_op jit(solution)/shard_map/reshape | solution.py:77
  88.7 35.2 %all-to-all-done.1 = bf16[8,256,512]{1,2,0:T(8,128)(2,1)S(1)} async-done(((bf16[8,256,512]{1,2,0:T(8,128)(2,1)}), bf16[8,256,512]{1,2,0:T(8,128)(2,1)S(1)}, u32[]{:S(2)}, u32[]{:S(2)}) %all-to-all-start.1) | async-done | bytes 2097184 | tf_op jit(solution)/shard_map/all_to_all | solution.py:72
  123.9 2.5 %copy.32 = bf16[8,256,512]{1,0,2:T(8,128)(2,1)} copy(bf16[8,256,512]{1,2,0:T(8,128)(2,1)S(1)} %all-to-all-done.1) | data formatting | bytes 4194304 | tf_op jit(solution)/shard_map/all_to_all | solution.py:72
  126.4 4.3 %reshape.103 = bf16[2048,8,64]{0,2,1:T(8,128)(2,1)} reshape(bf16[8,256,512]{1,0,2:T(8,128)(2,1)} %copy.32) | data formatting | bytes 4194304 | tf_op jit(solution)/shard_map/reshape | solution.py:76
  130.7 9.8 %while.14 = (s32[]{:T(128)}, f32[256,8,64]{0,2,1:T(8,128)S(1)}, bf16[2048,8,64]{0,2,1:T(8,128)(2,1)}, bf16[2048,8,64]{0,2,1:T(8,128)(2,1)}, bf16[256,8,64]{0,2,1...) while((s32[]{:T(128)}, f32[256,8,64]{0,2,1:T(8,128)S(1)}, ...), condition=%wide.region_6.7_spmd.clone, body=%wide.region_5.6_spmd.clone.sunk | while | flops 549715968 | bytes 3409556 | solution.py:87
  130.7 4.9 %fusion.48 = f32[256,8,64]{0,2,1:T(8,128)S(1)} fusion(bf16[256,8,64]{0,2,1:T(8,128)(2,1)S(1)} %get-tuple-element.188, bf16[2048,8,64]{0,2,1:T(8,128)(2,1)} %get-tuple-element.187, s32[]{:T(128)S(6)} %select_n.31, bf16[2048,8,64]{0,2,1:T(8,128)(2,1)} %get-tuple-element.186, f32[256,8,64]{0,2,1:T(8,128)S(1)} %get-tuple-element.176, pred[]{:T(512)S(6)} %compare.5), kind=kOutput, calls=%fused_computation.11.clone.1 | convolution fusion | flops 549715968 | bytes 3409408 | tf_op jit(solution)/shard_map/while/body/eval_jaxpr/...hck,...khd->...chd/dot_general | solution.py:23
  135.6 4.9 %fusion.48 = f32[256,8,64]{0,2,1:T(8,128)S(1)} fusion(bf16[256,8,64]{0,2,1:T(8,128)(2,1)S(1)} %get-tuple-element.188, bf16[2048,8,64]{0,2,1:T(8,128)(2,1)} %get-tuple-element.187, s32[]{:T(128)S(6)} %select_n.31, bf16[2048,8,64]{0,2,1:T(8,128)(2,1)} %get-tuple-element.186, f32[256,8,64]{0,2,1:T(8,128)S(1)} %get-tuple-element.176, pred[]{:T(512)S(6)} %compare.5), kind=kOutput, calls=%fused_computation.11.clone.1 | convolution fusion | flops 549715968 | bytes 3409408 | tf_op jit(solution)/shard_map/while/body/eval_jaxpr/...hck,...khd->...chd/dot_general | solution.py:23
  140.7 0.1 multiply_reduce_fusion
  140.8 0.2 copy.34
  141.0 0.6 copy-done.2
  141.6 0.2 copy-done.4
  141.8 1.1 convolution_convert_fusion
  (22 shorter events, 0.2 us)
Async XLA Ops:
  6.5 71.6 %copy-start = (bf16[512,1024]{1,0:T(8,128)(2,1)S(1)}, bf16[512,1024]{1,0:T(8,128)(2,1)}, u32[]{:S(2)}) copy-start(bf16[512,1024]{1,0:T(8,128)(2,1)} %param.14) | copy-start | bytes 3145732
  16.2 55.6 %all-to-all-start = ((bf16[8,256,512]{1,2,0:T(8,128)(2,1)}), bf16[8,256,512]{1,2,0:T(8,128)(2,1)}, u32[]{:S(2)}, u32[]{:S(2)}) async-start(bf16[8,256,512]{1,2,0:T(8,128)(2,1)} %copy.29), calls=%async_computation | async-start | bytes 4194304 | tf_op jit(solution)/shard_map/all_to_all | solution.py:73
  23.5 52.0 %all-gather.2.cloned.1.call-start = ((), (), s32[]{:S(2)}) async-start(), calls=%async_computation.2 | async-start | bytes 2621440 | tf_op jit(solution)/shard_map/all_gather | solution.py:35
  32.1 43.4 %copy-start.6 = (s32[256]{0:T(256)S(1)}, s32[256]{0:T(256)}, u32[]{:S(2)}) copy-start(s32[256]{0:T(256)} %param.10) | copy-start | bytes 3076
  71.8 52.1 %all-to-all-start.1 = ((bf16[8,256,512]{1,2,0:T(8,128)(2,1)}), bf16[8,256,512]{1,2,0:T(8,128)(2,1)S(1)}, u32[]{:S(2)}, u32[]{:S(2)}) async-start(bf16[8,256,512]{1,2,0:T(8,128)(2,1)} %copy.31), calls=%async_computation.1 | async-start | bytes 4194304 | tf_op jit(solution)/shard_map/all_to_all | solution.py:72
  78.7 0.8 copy-start.3
  126.4 4.3 %copy-start.1 = (f32[256,8,64]{0,2,1:T(8,128)S(1)}, f32[256,8,64]{0,2,1:T(8,128)}, u32[]{:S(2)}) copy-start(f32[256,8,64]{0,2,1:T(8,128)} %custom-call) | copy-start | bytes 1572868
  126.4 4.3 %copy-start.5 = (bf16[256,512]{0,1:T(8,128)(2,1)S(1)}, bf16[256,512]{0,1:T(8,128)(2,1)}, u32[]{:S(2)}) copy-start(bf16[256,512]{0,1:T(8,128)(2,1)} %copy.33) | copy-start | bytes 786436
  140.6 1.0 copy-start.2
  140.6 1.2 copy-start.4
Sparse Core Ops, SparseCore 0:
  25.9 23.9 all-gather.1
where the time goes:
time: 150 us
  waiting for transfers between devices  75.6 us (50%)
  local copies, waits for them, and re-layouts  33.4 us (22%)
  matrix products  13.8 us (9%)
  between operations  13.5 us (9%)
  starting transfers between devices  11 us (7%)
  other arithmetic  2.28 us (2%)
    all_to_all x1, waiting for transfers between devices, on_device(): lax.all_to_all(send_values, 'shard', split_axis=0, concat_axis=0, tiled=T...  39.7 us
    all_to_all x1, waiting for transfers between devices, on_device(): lax.all_to_all(send_keys, 'shard', split_axis=0, concat_axis=0, tiled=True)  35.2 us
    dot_general x2, matrix products, attend(): jnp.einsum('...hck,...khd->...chd', weight_low, value_rows, preferred_ele...  9.81 us
    all_to_all x1, starting transfers between devices, on_device(): lax.all_to_all(send_values, 'shard', split_axis=0, concat_axis=0, tiled=T...  7.28 us
    reshape x1, local copies, waits for them, and re-layouts, on_device(): all_keys = got_keys.reshape(key_count, head_count, head_size)  4.28 us
    reshape x1, local copies, waits for them, and re-layouts, on_device(): all_values = got_values.reshape(key_count, head_count, head_size)  4.2 us
    all_to_all x1, local copies, waits for them, and re-layouts, on_device(): lax.all_to_all(send_values, 'shard', split_axis=0, concat_axis=0, tiled=T...  4.09 us
    reshape x1, local copies, waits for them, and re-layouts, on_device(): padded_keys[source_block].reshape(peer_count, most_each * BLK, model_width)  3.92 us
  transfers between devices with their start and end apart: 3, of which 2 were waited for; matrix products, arithmetic and copies ran while one was open for 13% of the time, Pallas kernels for 0%

commit v1 on v0

v1 whole, which is shorter than its diff:
```python
import functools

import jax
import jax.numpy as jnp
from jax import lax
from jax.experimental import pallas as pl
from jax.experimental.pallas import tpu as pltpu
from jax.sharding import PartitionSpec as P

H = 8
BLK = 128
MOST = 2
PAIR = 128


def layer_norm(inputs):
    center = inputs - jnp.mean(inputs, axis=-1, keepdims=True)
    spread = jnp.mean(center * center, axis=-1, keepdims=True)
    return center * lax.rsqrt(spread + 1e-05)


def silu_of_half(half):
    return half + half * jnp.tanh(half)


def project(rows, weights):
    normed = layer_norm(rows.astype(jnp.float32)).astype(jnp.bfloat16)
    product = jnp.dot(normed, weights, preferred_element_type=jnp.float32)
    return silu_of_half(0.5 * product)


def select(index_column, table):
    rows = table.shape[0]
    ids = lax.broadcasted_iota(jnp.int32, (index_column.shape[0], rows), 1)
    one_hot = jnp.where(index_column == ids, 1.0, 0.0).astype(jnp.bfloat16)
    return jnp.dot(one_hot, table, preferred_element_type=jnp.float32).astype(jnp.bfloat16)


def partial_kernel(
    scorers, cand, dest_ref, inverse_ref, table_ref, w_ref, keys_ref, values_ref, out_ref,
    unique_ref, count_ref, slot_ref,
):
    width = table_ref.shape[1]
    head = width // H
    blocks = dest_ref.shape[0]
    chunk = 512

    @pl.loop(0, table_ref.shape[0] // chunk)
    def _(step):
        rows = pl.ds(pl.multiple_of(step * chunk, chunk), chunk)
        queries = project(table_ref[rows, :], w_ref[...]).astype(jnp.bfloat16)
        unique_ref[rows, :] = queries * jnp.bfloat16(0.5 / head**0.5)

    @pl.loop(0, scorers)
    def _(scorer):
        count_ref[scorer] = 0
        for slot in range(MOST):
            slot_ref[scorer * MOST + slot] = 0

    @pl.loop(0, blocks)
    def _(block):
        scorer = dest_ref[block]
        place = count_ref[scorer]
        slot_ref[scorer * MOST + place] = block
        count_ref[scorer] = place + 1

    lane = lax.broadcasted_iota(jnp.int32, (1, PAIR), 1)

    @pl.loop(0, scorers)
    def _(scorer):
        rows = pl.ds(pl.multiple_of(scorer * cand, cand), cand)
        count = count_ref[scorer]

        @pl.when(count == 0)
        def _():
            out_ref[rows, :] = jnp.zeros((cand, width), out_ref.dtype)

        @pl.when(count > 0)
        def _():
            queries = select(inverse_ref[rows, :], unique_ref[...])
            second = jnp.where(count > 1, 1.0, 0.0).astype(jnp.bfloat16)
            first_block, second_block = slot_ref[scorer * MOST], slot_ref[scorer * MOST + 1]
            for pair in range(width // PAIR):
                at = slice(pair * PAIR, (pair + 1) * PAIR)
                keys = jnp.concatenate(
                    [keys_ref[first_block, :, at], keys_ref[second_block, :, at] * second], axis=0
                )
                values = jnp.concatenate(
                    [values_ref[first_block, :, at], values_ref[second_block, :, at]], axis=0
                )
                total = jnp.zeros((cand, PAIR), jnp.float32)
                for inner in range(PAIR // head):
                    own = jnp.where(lane // head == inner, 1.0, 0.0).astype(jnp.bfloat16)
                    half = lax.dot_general(
                        queries[:, at] * own, keys, (((1,), (1,)), ((), ())),
                        preferred_element_type=jnp.float32,
                    )
                    weight = silu_of_half(half).astype(jnp.bfloat16)
                    total += jnp.dot(weight, values * own, preferred_element_type=jnp.float32)
                out_ref[rows, at] = total.astype(out_ref.dtype)


def gate_kernel(inverse_ref, table_ref, w_ref, gate_ref):
    gate_ref[...] = project(select(inverse_ref[...], table_ref[...]), w_ref[...]).astype(gate_ref.dtype)


def final_kernel(attended_ref, gate_ref, w_ref, out_ref):
    gated = layer_norm(attended_ref[...].astype(jnp.float32)) * gate_ref[...].astype(jnp.float32)
    out_ref[...] = jnp.dot(
        gated.astype(jnp.bfloat16), w_ref[...], preferred_element_type=jnp.float32
    ).astype(out_ref.dtype)


VMEM = pl.BlockSpec(memory_space=pltpu.VMEM)
SMEM = pl.BlockSpec(memory_space=pltpu.SMEM)


def on_device(cand_table, inverse, cache_keys, cache_values, block_dest, w_in, w_out):
    width = w_out.shape[0]
    cand = inverse.shape[0]
    scorers = lax.axis_size("shard")
    blocks = block_dest.shape[0]
    table = lax.all_gather(cand_table, "grp", axis=0, tiled=True)
    every_inverse = lax.all_gather(inverse, "shard", axis=0, tiled=True)
    unique = table.shape[0]
    partial = pl.pallas_call(
        functools.partial(partial_kernel, scorers, cand),
        out_shape=jax.ShapeDtypeStruct((scorers * cand, width), jnp.bfloat16),
        in_specs=[SMEM, VMEM, VMEM, VMEM, VMEM, VMEM],
        out_specs=VMEM,
        scratch_shapes=[
            pltpu.VMEM((unique, width), jnp.bfloat16),
            pltpu.SMEM((scorers,), jnp.int32),
            pltpu.SMEM((scorers * MOST,), jnp.int32),
        ],
        compiler_params=pltpu.CompilerParams(vmem_limit_bytes=48 * 2**20),
        name="partial_sums",
    )(
        block_dest[:, 0],
        every_inverse[:, None],
        table,
        w_in[:, width:],
        cache_keys.reshape(blocks, BLK, width),
        cache_values.reshape(blocks, BLK, width),
    )
    attended = lax.psum_scatter(partial, "shard", scatter_dimension=0, tiled=True)
    gate = pl.pallas_call(
        gate_kernel,
        out_shape=jax.ShapeDtypeStruct((cand, width), jnp.bfloat16),
        in_specs=[VMEM] * 3,
        out_specs=VMEM,
        compiler_params=pltpu.CompilerParams(vmem_limit_bytes=32 * 2**20),
        cost_estimate=pl.CostEstimate(
            flops=2 * cand * width * (unique + width), bytes_accessed=2 * unique * width, transcendentals=0
        ),
        name="gate",
    )(inverse[:, None], table, w_in[:, :width])
    return pl.pallas_call(
        final_kernel,
        out_shape=jax.ShapeDtypeStruct((cand, width), jnp.bfloat16),
        in_specs=[VMEM] * 3,
        out_specs=VMEM,
        name="final",
    )(attended, gate, w_out)


def solution(mesh):
    rows = P(("grp", "shard"), None)
    in_specs = (P("grp", None), P(("grp", "shard")), rows, rows, rows, P(), P())
    return jax.shard_map(
        on_device, mesh=mesh, in_specs=in_specs, out_specs=rows, check_vma=False
    )
```

time: 150 us -> 134 us (0.89)
  local copies, waits for them, and re-layouts: 33.4 us -> 5.62 us
  Pallas kernels: 0 us -> 23 us
  blocking collectives: 0 us -> 22.5 us
  matrix products: 13.8 us -> 0 us
  starting transfers between devices: 11 us -> 0.04 us
  waiting for transfers between devices: 75.6 us -> 68.9 us
  other arithmetic: 2.28 us -> 0 us
    all_to_all x2 -> x0, waiting for transfers between devices: 74.9 us -> none  [the longest x1 39.7 us: on_device(): lax.all_to_all(send_values, 'shard', split_axis=0, concat_axis=0, tiled=T...]
    reduce_scatter x0 -> x1, waiting for transfers between devices: none -> 64.3 us  [on_device(): lax.psum_scatter(partial, 'shard', scatter_dimension=0, tiled=True)]
    pallas_call x0 -> x3, Pallas kernels: none -> 23 us  [the longest x1 19.4 us: on_device(): pl.pallas_call(functools.partial(partial_kernel, scorers, cand), out_shap...]
    all_gather x0 -> x1, blocking collectives: none -> 22.5 us  [on_device(): every_inverse = lax.all_gather(inverse, 'shard', axis=0, tiled=True)]
    reshape x5 -> x0, local copies, waits for them, and re-layouts: 16.5 us -> none  [the longest x1 4.28 us: on_device(): all_keys = got_keys.reshape(key_count, head_count, head_size)]
    dot_general x5 -> x0, matrix products: 13.8 us -> none  [the longest x2 9.81 us: attend(): jnp.einsum('...hck,...khd->...chd', weight_low, value_rows, preferred_ele...]
    all_to_all x2 -> x0, starting transfers between devices: 10.9 us -> none  [the longest x1 7.28 us: on_device(): lax.all_to_all(send_values, 'shard', split_axis=0, concat_axis=0, tiled=T...]
    all_to_all x2 -> x0, local copies, waits for them, and re-layouts: 6.6 us -> none  [the longest x1 4.09 us: on_device(): lax.all_to_all(send_values, 'shard', split_axis=0, concat_axis=0, tiled=T...]
  transfers between devices with their start and end apart: 3 -> 2, of which waited for: 2 -> 2; matrix products, arithmetic and copies ran while one was open for 13% -> 0% of each run, Pallas kernels for 0% -> 1%
where the time goes in v1:
time: 134 us
  waiting for transfers between devices  68.9 us (51%)
  Pallas kernels  23 us (17%)
  blocking collectives  22.5 us (17%)
  between operations  13.5 us (10%)
  local copies, waits for them, and re-layouts  5.62 us (4%)
    reduce_scatter x1, waiting for transfers between devices, on_device(): lax.psum_scatter(partial, 'shard', scatter_dimension=0, tiled=True)  64.3 us
    all_gather x1, blocking collectives, on_device(): every_inverse = lax.all_gather(inverse, 'shard', axis=0, tiled=True)  22.5 us
    pallas_call x1, Pallas kernels, on_device(): pl.pallas_call(functools.partial(partial_kernel, scorers, cand), out_shap...  19.4 us
    unnamed x14, local copies, waits for them, and re-layouts  5.05 us
    all_gather x1, waiting for transfers between devices, on_device(): table = lax.all_gather(cand_table, 'grp', axis=0, tiled=True)  3.95 us
  transfers between devices with their start and end apart: 2, of which 2 were waited for; matrix products, arithmetic and copies ran while one was open for 0% of the time, Pallas kernels for 1%

profile of v1, /device:TPU:0, one launch (start us, length us, event | category | flops | bytes accessed | tf_op | source)
XLA Modules:
  0.0 133.6 jit_solution(3188953747168199422)
XLA Ops:
  6.5 0.0 copy-start.5
  6.5 0.0 copy-start.4
  6.5 0.0 all-gather.3.cloned.1.call-start
  6.5 0.7 all-gather.3.cloned.1.call-update
  7.3 0.0 reduce-scatter.2.cloned.1.call-start
  7.3 22.5 %all-gather = s32[8,1,256]{2,1,0:T(1,128)S(1)} all-gather(s32[1,1,256]{2,1,0:T(1,128)} %bitcast.10), channel_id=1, replica_groups=mesh['grp'=4,'shard'=8] {'shard'}, dimensions={0}, use_global_device_ids=true | all-gather | bytes 9216 | tf_op jit(solution)/shard_map/all_gather | solution.py:124
  29.8 0.4 copy.10.inverse_ref
  30.2 0.0 copy-done.5
  30.2 0.1 fusion
  30.3 4.0 %all-gather.3.cloned.1.call-done.table_ref = bf16[2048,512]{1,0:T(8,128)(2,1)} async-done(((bf16[512,512]{1,0:T(8,128)(2,1)}), bf16[2048,512]{1,0:T(8,128)(2,1)}) %all-gather.3.cloned.1.call-update) | async-done | bytes 2097168 | tf_op jit(solution)/shard_map/all_gather | solution.py:123
  34.2 0.0 copy-done.4
  34.2 0.0 copy-start
  34.2 1.6 %copy-done = bf16[2048,512]{1,0:T(8,128)(2,1)S(1)} copy-done((bf16[2048,512]{1,0:T(8,128)(2,1)S(1)}, bf16[2048,512]{1,0:T(8,128)(2,1)}, u32[]{:S(2)}) %copy-start) | copy-done | bytes 2097176
  35.8 19.4 %partial_sums.1 = bf16[2048,512]{1,0:T(8,128)(2,1)S(1)} custom-call(s32[16]{0:T(128)S(1)} %bitcast.6, s32[2048,1]{1,0:T(8,128)S(1)} %copy.10.inverse_ref, bf16[2048,512]{1,0:T(8,128)(2,1)S(1)} %copy-done, bf16[512,512]{1,0:T(8,128)(2,1)S(1)} %get-tuple-element.6.w_ref, bf16[16,128,512]{2,1,0:T(8,128)(2,1)} %bitcast.7, bf16[16,128,512]{2,1,0:T(8,128)(2,1)} %bitcast.8), custom_call_target="tpu_custom_call" | custom-call | tf_op jit(solution)/shard_map/partial_sums/pallas_call | solution.py:126
  55.2 0.0 copy-start.2
  55.2 1.3 copy-done.2
  56.6 0.0 copy-start.6
  56.6 0.0 copy-start.1
  56.6 0.0 reduce-scatter.2.cloned.1.call-update
  56.6 0.7 copy-done.6
  57.2 0.1 copy.11.inverse_ref
  57.4 0.8 copy-done.1
  58.2 1.2 gate.1.gate_ref
  59.4 0.0 copy-start.3
  59.4 0.7 copy-done.3
  60.0 64.3 %reduce-scatter.2.cloned.1.call-done.attended_ref = bf16[256,512]{1,0:T(8,128)(2,1)} async-done(((bf16[2048,512]{1,0:T(8,128)(2,1)}), bf16[256,512]{1,0:T(8,128)(2,1)}) %reduce-scatter.2.cloned.1.call-update) | async-done | bytes 262160 | tf_op jit(solution)/shard_map/reduce_scatter | solution.py:146
  124.3 2.4 %final.1 = bf16[256,512]{1,0:T(8,128)(2,1)} custom-call(bf16[256,512]{1,0:T(8,128)(2,1)} %reduce-scatter.2.cloned.1.call-done.attended_ref, bf16[256,512]{1,0:T(8,128)(2,1)} %copy-done.3, bf16[512,512]{1,0:T(8,128)(2,1)} %w_ref.1), custom_call_target="tpu_custom_call" | custom-call | tf_op jit(solution)/shard_map/final/pallas_call | solution.py:158
Async XLA Ops:
  6.5 23.7 %copy-start.5 = (bf16[512,1024]{1,0:T(8,128)(2,1)S(1)}, bf16[512,1024]{1,0:T(8,128)(2,1)}, u32[]{:S(2)}) copy-start(bf16[512,1024]{1,0:T(8,128)(2,1)} %param.12) | copy-start | bytes 3145732
  6.5 27.7 %copy-start.4 = (s32[16,1]{0,1:T(1,128)S(1)}, s32[16,1]{0,1:T(1,128)}, u32[]{:S(2)}) copy-start(s32[16,1]{0,1:T(1,128)} %param.11) | copy-start | bytes 196
  6.5 27.7 %all-gather.3.cloned.1.call-start = ((), (), s32[]{:S(2)}) async-start(), calls=%async_computation.1 | async-start | bytes 2621440 | tf_op jit(solution)/shard_map/all_gather | solution.py:123
  7.3 117.1 %reduce-scatter.2.cloned.1.call-start = ((), (), s32[]{:S(2)}) async-start(), calls=%async_computation.2 | async-start | bytes 2359296 | tf_op jit(solution)/shard_map/reduce_scatter | solution.py:146
  34.2 1.6 %copy-start = (bf16[2048,512]{1,0:T(8,128)(2,1)S(1)}, bf16[2048,512]{1,0:T(8,128)(2,1)}, u32[]{:S(2)}) copy-start(bf16[2048,512]{1,0:T(8,128)(2,1)} %all-gather.3.cloned.1.call-done.table_ref) | copy-start | bytes 6291460
  55.2 1.3 copy-start.2
  56.6 0.7 copy-start.6
  56.6 1.6 %copy-start.1 = (bf16[2048,512]{1,0:T(8,128)(2,1)S(1)}, bf16[2048,512]{1,0:T(8,128)(2,1)}, u32[]{:S(2)}) copy-start(bf16[2048,512]{1,0:T(8,128)(2,1)} %all-gather.3.cloned.1.call-done.table_ref) | copy-start | bytes 6291460
  59.4 0.7 copy-start.3
Sparse Core Ops, SparseCore 0:
  8.9 25.2 all-gather.2
  56.7 67.5 reduce-scatter.1

commit v2 on v1

--- a/solution.py
+++ b/solution.py
@@ -104,11 +104,115 @@
     gate_ref[...] = project(select(inverse_ref[...], table_ref[...]), w_ref[...]).astype(gate_ref.dtype)
 
 
-def final_kernel(attended_ref, gate_ref, w_ref, out_ref):
-    gated = layer_norm(attended_ref[...].astype(jnp.float32)) * gate_ref[...].astype(jnp.float32)
+def send(source, target, send_sem, recv_sem, **device):
+    copy = pltpu.make_async_remote_copy(
+        src_ref=source, dst_ref=target, send_sem=send_sem, recv_sem=recv_sem,
+        device_id=device, device_id_type=pl.DeviceIdType.MESH,
+    )
+    copy.start()
+    return copy
+
+
+def greet(devices):
+    barrier = pltpu.get_barrier_semaphore()
+    for device in devices:
+        pl.semaphore_signal(
+            barrier, inc=1, device_id=device, device_id_type=pl.DeviceIdType.MESH
+        )
+    pl.semaphore_wait(barrier, len(devices))
+
+
+def gather_kernel(
+    groups, scorers, own_ref, inverse_ref, table_ref, every_ref,
+    keep_sem, far_send, far_recv, near_send, near_recv, index_send, index_recv,
+):
+    group, scorer = lax.axis_index("grp"), lax.axis_index("shard")
+    chips = groups // 2
+    chip, core = group // 2, group % 2
+    other_core = chip * 2 + 1 - core
+    far = {k: lax.rem(chip + k, chips) * 2 + core for k in range(1, chips)}
+    from_far = {k: lax.rem(chip + chips - k, chips) * 2 + core for k in range(1, chips)}
+    peers = {k: lax.rem(scorer + k, scorers) for k in range(1, scorers)}
+    greet(
+        [{"grp": g} for g in far.values()] + [{"grp": other_core}]
+        + [{"shard": s} for s in peers.values()]
+    )
+    copies = [
+        send(own_ref, table_ref.at[group], far_send.at[k], far_recv.at[k], grp=far[k])
+        for k in far
+    ]
+    copies += [
+        send(inverse_ref, every_ref.at[scorer], index_send.at[k], index_recv.at[k], shard=peers[k])
+        for k in peers
+    ]
+    relays = [
+        send(own_ref, table_ref.at[group], near_send.at[0], near_recv.at[0], grp=other_core)
+    ]
+    keep = pltpu.make_async_copy(own_ref, table_ref.at[group], keep_sem)
+    keep.start()
+    every_ref[scorer] = inverse_ref[...]
+    for k, copy in zip(far, copies):
+        copy.wait_recv()
+        block = table_ref.at[from_far[k]]
+        relays.append(
+            send(block, block, near_send.at[k], near_recv.at[k], grp=other_core)
+        )
+    keep.wait()
+    for copy in copies:
+        copy.wait_send()
+    for copy in copies[len(far):]:
+        copy.wait_recv()
+    for copy in relays:
+        copy.wait()
+
+
+def reduce_kernel(
+    scorers, cand, partial_ref, gate_ref, w_ref, out_ref, pair_ref, sum_ref, got_ref,
+    pair_send, pair_recv, far_send, far_recv,
+):
+    me = lax.axis_index("shard")
+    places = scorers // 2
+    place, side = me // 2, me % 2
+    partner = place * 2 + 1 - side
+    target = {k: lax.rem(place + k, places) for k in range(places)}
+    greet([{"shard": partner}] + [{"shard": target[k] * 2 + side} for k in range(1, places)])
+
+    def rows(scorer):
+        return pl.ds(pl.multiple_of(scorer * cand, cand), cand)
+
+    order = [*range(places // 2, places), *range(1, places // 2), 0]
+    pairs = {
+        k: send(
+            partial_ref.at[rows(target[k] * 2 + 1 - side)], pair_ref.at[k],
+            pair_send.at[k], pair_recv.at[k], shard=partner,
+        )
+        for k in order
+    }
+    far = []
+    for k in order:
+        pairs[k].wait_recv()
+        total = partial_ref[rows(target[k] * 2 + side), :].astype(jnp.float32) + pair_ref[k].astype(
+            jnp.float32
+        )
+        if k:
+            sum_ref[k] = total.astype(sum_ref.dtype)
+            far.append(
+                send(
+                    sum_ref.at[k], got_ref.at[k], far_send.at[k], far_recv.at[k],
+                    shard=target[k] * 2 + side,
+                )
+            )
+    for k, copy in zip(order, far):
+        copy.wait_recv()
+        total += got_ref[k].astype(jnp.float32)
+    gated = layer_norm(total) * gate_ref[...].astype(jnp.float32)
     out_ref[...] = jnp.dot(
         gated.astype(jnp.bfloat16), w_ref[...], preferred_element_type=jnp.float32
     ).astype(out_ref.dtype)
+    for k in order:
+        pairs[k].wait_send()
+    for copy in far:
+        copy.wait_send()
 
 
 VMEM = pl.BlockSpec(memory_space=pltpu.VMEM)
@@ -120,8 +224,27 @@
     cand = inverse.shape[0]
     scorers = lax.axis_size("shard")
     blocks = block_dest.shape[0]
-    table = lax.all_gather(cand_table, "grp", axis=0, tiled=True)
-    every_inverse = lax.all_gather(inverse, "shard", axis=0, tiled=True)
+    groups = lax.axis_size("grp")
+    dma = pltpu.SemaphoreType.DMA
+    table, every_inverse = pl.pallas_call(
+        functools.partial(gather_kernel, groups, scorers),
+        out_shape=(
+            jax.ShapeDtypeStruct((groups, *cand_table.shape), cand_table.dtype),
+            jax.ShapeDtypeStruct((scorers, 1, cand), inverse.dtype),
+        ),
+        in_specs=[VMEM] * 2,
+        out_specs=(VMEM, VMEM),
+        scratch_shapes=[
+            dma, dma((groups // 2,)), dma((groups // 2,)), dma((groups // 2,)), dma((groups // 2,)),
+            dma((scorers,)), dma((scorers,)),
+        ],
+        compiler_params=pltpu.CompilerParams(
+            collective_id=0, has_side_effects=True, vmem_limit_bytes=24 * 2**20
+        ),
+        name="gather",
+    )(cand_table, inverse[None, :])
+    table = table.reshape(-1, width)
+    every_inverse = every_inverse.reshape(-1)
     unique = table.shape[0]
     partial = pl.pallas_call(
         functools.partial(partial_kernel, scorers, cand),
@@ -143,7 +266,6 @@
         cache_keys.reshape(blocks, BLK, width),
         cache_values.reshape(blocks, BLK, width),
     )
-    attended = lax.psum_scatter(partial, "shard", scatter_dimension=0, tiled=True)
     gate = pl.pallas_call(
         gate_kernel,
         out_shape=jax.ShapeDtypeStruct((cand, width), jnp.bfloat16),
@@ -155,13 +277,18 @@
         ),
         name="gate",
     )(inverse[:, None], table, w_in[:, :width])
+    places = scorers // 2
     return pl.pallas_call(
-        final_kernel,
+        functools.partial(reduce_kernel, scorers, cand),
         out_shape=jax.ShapeDtypeStruct((cand, width), jnp.bfloat16),
         in_specs=[VMEM] * 3,
         out_specs=VMEM,
-        name="final",
-    )(attended, gate, w_out)
+        scratch_shapes=[pltpu.VMEM((places, cand, width), jnp.bfloat16)] * 3 + [dma((places,))] * 4,
+        compiler_params=pltpu.CompilerParams(
+            collective_id=1, has_side_effects=True, vmem_limit_bytes=40 * 2**20
+        ),
+        name="reduce",
+    )(partial, gate, w_out)
 
 
 def solution(mesh):

time: 134 us -> 78.5 us (0.59)
  waiting for transfers between devices: 68.9 us -> 0 us
  Pallas kernels: 23 us -> 73.2 us
  blocking collectives: 22.5 us -> 0 us
  between operations: 13.5 us -> 0.08 us
    reduce_scatter x1 -> x0, waiting for transfers between devices: 64.3 us -> none  [on_device(): lax.psum_scatter(partial, 'shard', scatter_dimension=0, tiled=True)]
    pallas_call x1 -> x2, Pallas kernels: 2.39 us -> 52.7 us  [the longest x1 31.8 us: on_device(): pl.pallas_call(functools.partial(reduce_kernel, scorers, cand), out_shape...]
    all_gather x1 -> x0, blocking collectives: 22.5 us -> none  [on_device(): every_inverse = lax.all_gather(inverse, 'shard', axis=0, tiled=True)]
    all_gather x1 -> x0, waiting for transfers between devices: 3.95 us -> none  [on_device(): table = lax.all_gather(cand_table, 'grp', axis=0, tiled=True)]
    unnamed x14 -> x11, local copies, waits for them, and re-layouts: 5.05 us -> 1.76 us
    slice x1, local copies, waits for them, and re-layouts: 0.08 us -> 2.07 us  [on_device(): w_in[:, :width]]
  transfers between devices with their start and end apart: 2 -> 0, of which waited for: 2 -> 0; matrix products, arithmetic and copies ran while one was open for 0% -> 0% of each run, Pallas kernels for 1% -> 0%
where the time goes in v2:
time: 78.5 us; the launch traced here: 78.4 us
  Pallas kernels  73.2 us (93%)
  local copies, waits for them, and re-layouts  5.06 us (6%)
    pallas_call x1, Pallas kernels, on_device(): pl.pallas_call(functools.partial(reduce_kernel, scorers, cand), out_shape...  31.8 us
    pallas_call x1, Pallas kernels, on_device(): pl.pallas_call(functools.partial(gather_kernel, groups, scorers), out_sha...  20.9 us
    pallas_call x1, Pallas kernels, on_device(): pl.pallas_call(functools.partial(partial_kernel, scorers, cand), out_shap...  19.3 us
    slice x1, local copies, waits for them, and re-layouts, on_device(): w_in[:, :width]  2.07 us
    unnamed x11, local copies, waits for them, and re-layouts  1.76 us

profile of v2, /device:TPU:0, one launch (start us, length us, event | category | flops | bytes accessed | tf_op | source)
XLA Modules:
  0.0 78.4 jit_solution(16806476311532746103)
XLA Ops:
  0.0 0.0 copy-start.3
  0.0 0.0 copy-start.1
  0.0 0.9 %copy.9.inverse_ref = s32[256,1]{1,0:T(8,128)S(1)} copy(s32[256,1]{0,1:T(1,128)} %bitcast.10) | data formatting | bytes 2048 | tf_op jit(solution)/shard_map/broadcast_in_dim | solution.py:279
  0.9 2.1 %fusion = (bf16[512,512]{1,0:T(8,128)(2,1)S(1)}, bf16[512,512]{1,0:T(8,128)(2,1)}) fusion(bf16[512,1024]{1,0:T(8,128)(2,1)} %param.12), kind=kLoop, calls=%fused_computation | loop fusion | bytes 2097152 | tf_op jit(solution)/shard_map/slice | solution.py:279
  3.0 0.0 copy-done.3
  3.0 0.0 copy-done.1
  3.0 20.9 %gather.1 = (bf16[4,512,512]{2,1,0:T(8,128)(2,1)S(1)}, s32[8,1,256]{2,1,0:T(1,128)S(1)}) custom-call(bf16[512,512]{1,0:T(8,128)(2,1)S(1)} %copy-done.1, s32[1,256]{1,0:T(1,128)S(1)} %bitcast.11), custom_call_target="tpu_custom_call" | custom-call | tf_op jit(solution)/shard_map/gather/pallas_call | solution.py:229
  23.9 0.0 copy-start.4
  23.9 1.2 %gate.1.gate_ref = bf16[256,512]{1,0:T(8,128)(2,1)S(1)} custom-call(s32[256,1]{1,0:T(8,128)S(1)} %copy.9.inverse_ref, bf16[2048,512]{1,0:T(8,128)(2,1)S(1)} %bitcast.7, bf16[512,512]{1,0:T(8,128)(2,1)S(1)} %get-tuple-element.9.w_ref), custom_call_target="tpu_custom_call" | custom-call | flops 671088640 | bytes 2097152 | tf_op jit(solution)/shard_map/gate/pallas_call | solution.py:269
  25.1 0.4 copy.8.inverse_ref
  25.4 0.0 copy-done.4
  25.4 0.0 copy-start
  25.5 1.0 %copy-done = bf16[512,512]{1,0:T(8,128)(2,1)S(1)} copy-done((bf16[512,512]{1,0:T(8,128)(2,1)S(1)}, bf16[512,512]{1,0:T(8,128)(2,1)}, u32[]{:S(2)}) %copy-start) | copy-done | bytes 524312
  26.5 0.0 copy-start.2
  26.5 19.3 %partial_sums.1.partial_ref = bf16[2048,512]{1,0:T(8,128)(2,1)S(1)} custom-call(s32[16]{0:T(128)S(1)} %bitcast.12, s32[2048,1]{1,0:T(8,128)S(1)} %copy.8.inverse_ref, bf16[2048,512]{1,0:T(8,128)(2,1)S(1)} %bitcast.8, bf16[512,512]{1,0:T(8,128)(2,1)S(1)} %copy-done, bf16[16,128,512]{2,1,0:T(8,128)(2,1)} %bitcast.13, bf16[16,128,512]{2,1,0:T(8,128)(2,1)} %bitcast.14), custom_call_target="tpu_custom_call" | custom-call | tf_op jit(solution)/shard_map/partial_sums/pallas_call | solution.py:249
  45.8 0.0 copy-done.2
  45.8 31.8 %reduce.1 = bf16[256,512]{1,0:T(8,128)(2,1)S(1)} custom-call(bf16[2048,512]{1,0:T(8,128)(2,1)S(1)} %partial_sums.1.partial_ref, bf16[256,512]{1,0:T(8,128)(2,1)S(1)} %gate.1.gate_ref, bf16[512,512]{1,0:T(8,128)(2,1)S(1)} %copy-done.2), custom_call_target="tpu_custom_call" | custom-call | tf_op jit(solution)/shard_map/reduce/pallas_call | solution.py:281
  77.6 0.7 copy.11
Async XLA Ops:
  0.0 3.0 %copy-start.3 = (s32[256]{0:T(256)S(1)}, s32[256]{0:T(256)}, u32[]{:S(2)}) copy-start(s32[256]{0:T(256)} %param.8) | copy-start | bytes 3076
  0.0 3.0 %copy-start.1 = (bf16[512,512]{1,0:T(8,128)(2,1)S(1)}, bf16[512,512]{1,0:T(8,128)(2,1)}, u32[]{:S(2)}) copy-start(bf16[512,512]{1,0:T(8,128)(2,1)} %own_ref.1) | copy-start | bytes 1572868
  23.9 1.6 %copy-start.4 = (s32[16,1]{0,1:T(1,128)S(1)}, s32[16,1]{0,1:T(1,128)}, u32[]{:S(2)}) copy-start(s32[16,1]{0,1:T(1,128)} %param.11) | copy-start | bytes 196
  25.4 1.0 %copy-start = (bf16[512,512]{1,0:T(8,128)(2,1)S(1)}, bf16[512,512]{1,0:T(8,128)(2,1)}, u32[]{:S(2)}) copy-start(bf16[512,512]{1,0:T(8,128)(2,1)} %get-tuple-element.10.w_ref) | copy-start | bytes 1572868
  26.5 19.3 %copy-start.2 = (bf16[512,512]{1,0:T(8,128)(2,1)S(1)}, bf16[512,512]{1,0:T(8,128)(2,1)}, u32[]{:S(2)}) copy-start(bf16[512,512]{1,0:T(8,128)(2,1)} %w_ref.1) | copy-start | bytes 1572868

commit v3 on v2

v3 whole, which is shorter than its diff:
```python
import functools

import jax
import jax.numpy as jnp
from jax import lax
from jax.experimental import pallas as pl
from jax.experimental.pallas import tpu as pltpu
from jax.sharding import PartitionSpec as P

H = 8
BLK = 128
MOST = 2
PAIR = 128


def layer_norm(inputs):
    center = inputs - jnp.mean(inputs, axis=-1, keepdims=True)
    spread = jnp.mean(center * center, axis=-1, keepdims=True)
    return center * lax.rsqrt(spread + 1e-05)


def silu_of_half(half):
    return half + half * jnp.tanh(half)


def project(rows, weights):
    normed = layer_norm(rows.astype(jnp.float32)).astype(jnp.bfloat16)
    product = jnp.dot(normed, weights, preferred_element_type=jnp.float32)
    return silu_of_half(0.5 * product)


def select(index_column, table):
    rows = table.shape[0]
    ids = lax.broadcasted_iota(jnp.int32, (index_column.shape[0], rows), 1)
    one_hot = jnp.where(index_column == ids, 1.0, 0.0).astype(jnp.bfloat16)
    return jnp.dot(one_hot, table, preferred_element_type=jnp.float32).astype(jnp.bfloat16)


def arrange_kernel(scorers, dest_ref, keys_ref, values_ref, out_keys_ref, out_values_ref, count_ref, sems):
    @pl.loop(0, scorers)
    def _(scorer):
        count_ref[scorer] = 0

    @pl.loop(0, dest_ref.shape[0])
    def _(block):
        scorer = dest_ref[block]
        place = count_ref[scorer]
        rows = pl.ds(pl.multiple_of(place * BLK, BLK), BLK)
        count_ref[scorer] = place + 1
        pltpu.make_async_copy(keys_ref.at[block], out_keys_ref.at[scorer, rows], sems.at[0, block]).start()
        pltpu.make_async_copy(values_ref.at[block], out_values_ref.at[scorer, rows], sems.at[1, block]).start()

    @pl.loop(0, scorers)
    def _(scorer):
        for place in range(MOST):
            @pl.when(count_ref[scorer] <= place)
            def _():
                rows = pl.ds(place * BLK, BLK)
                empty = jnp.zeros((BLK, keys_ref.shape[2]), out_keys_ref.dtype)
                out_keys_ref[scorer, rows, :] = empty
                out_values_ref[scorer, rows, :] = empty

    @pl.loop(0, dest_ref.shape[0])
    def _(block):
        rows = pl.ds(0, BLK)
        pltpu.make_async_copy(keys_ref.at[block], out_keys_ref.at[0, rows], sems.at[0, block]).wait()
        pltpu.make_async_copy(values_ref.at[block], out_values_ref.at[0, rows], sems.at[1, block]).wait()


def attend(queries, keys_ref, values_ref, scorer, out_ref, rows):
    width = queries.shape[1]
    head = width // H
    lane = lax.broadcasted_iota(jnp.int32, (1, PAIR), 1)
    for pair in range(width // PAIR):
        at = slice(pair * PAIR, (pair + 1) * PAIR)
        keys, values = keys_ref[scorer, :, at], values_ref[scorer, :, at]
        total = jnp.zeros((queries.shape[0], PAIR), jnp.float32)
        for inner in range(PAIR // head):
            own = jnp.where(lane // head == inner, 1.0, 0.0).astype(jnp.bfloat16)
            half = lax.dot_general(
                queries[:, at] * own, keys, (((1,), (1,)), ((), ())),
                preferred_element_type=jnp.float32,
            )
            weight = silu_of_half(half).astype(jnp.bfloat16)
            total += jnp.dot(weight, values * own, preferred_element_type=jnp.float32)
        out_ref[rows, at] = total.astype(out_ref.dtype)


def send(source, target, send_sem, recv_sem, **device):
    copy = pltpu.make_async_remote_copy(
        src_ref=source, dst_ref=target, send_sem=send_sem, recv_sem=recv_sem,
        device_id=device, device_id_type=pl.DeviceIdType.MESH,
    )
    copy.start()
    return copy


def greet(devices):
    barrier = pltpu.get_barrier_semaphore()
    for device in devices:
        pl.semaphore_signal(
            barrier, inc=1, device_id=device, device_id_type=pl.DeviceIdType.MESH
        )
    pl.semaphore_wait(barrier, len(devices))


def gather_kernel(
    groups, scorers, own_ref, inverse_ref, w_ref, table_ref, every_ref, unique_ref,
    keep_sem, far_send, far_recv, near_send, near_recv, index_send, index_recv,
):
    group, scorer = lax.axis_index("grp"), lax.axis_index("shard")
    chips = groups // 2
    chip, core = group // 2, group % 2
    other_core = chip * 2 + 1 - core
    far = {k: lax.rem(chip + k, chips) * 2 + core for k in range(1, chips)}
    from_far = {k: lax.rem(chip + chips - k, chips) * 2 + core for k in range(1, chips)}
    peers = {k: lax.rem(scorer + k, scorers) for k in range(1, scorers)}
    greet(
        [{"grp": g} for g in far.values()] + [{"grp": other_core}]
        + [{"shard": s} for s in peers.values()]
    )
    copies = [
        send(own_ref, table_ref.at[group], far_send.at[k], far_recv.at[k], grp=far[k])
        for k in far
    ]
    copies += [
        send(inverse_ref, every_ref.at[scorer], index_send.at[k], index_recv.at[k], shard=peers[k])
        for k in peers
    ]
    relays = [
        send(own_ref, table_ref.at[group], near_send.at[0], near_recv.at[0], grp=other_core)
    ]
    keep = pltpu.make_async_copy(own_ref, table_ref.at[group], keep_sem)
    keep.start()
    every_ref[scorer] = inverse_ref[...]

    def project_rows(block, rows):
        width = w_ref.shape[0]
        queries = project(rows, w_ref[:, width:]).astype(jnp.bfloat16)
        unique_ref[block] = queries * jnp.bfloat16(0.5 / (width // H) ** 0.5)

    project_rows(group, own_ref[...])
    relays[0].wait_recv()
    project_rows(other_core, table_ref[other_core])
    for k, copy in zip(far, copies):
        copy.wait_recv()
        block = table_ref.at[from_far[k]]
        relays.append(
            send(block, block, near_send.at[k], near_recv.at[k], grp=other_core)
        )
        project_rows(from_far[k], table_ref[from_far[k]])
        relays[k].wait_recv()
        twin = from_far[k] + 1 - 2 * core
        project_rows(twin, table_ref[twin])
    keep.wait()
    for copy in copies:
        copy.wait_send()
    for copy in copies[len(far):]:
        copy.wait_recv()
    for copy in relays:
        copy.wait_send()


def reduce_kernel(
    scorers, cand, inverse_ref, unique_ref, keys_ref, values_ref, table_ref, w_in_ref, w_out_ref, out_ref,
    partial_ref, pair_ref, sum_ref, got_ref, pair_send, pair_recv, far_send, far_recv,
):
    me = lax.axis_index("shard")
    width = w_out_ref.shape[0]
    places = scorers // 2
    place, side = me // 2, me % 2
    partner = place * 2 + 1 - side
    greet(
        [{"shard": partner}]
        + [{"shard": lax.rem(place + k, places) * 2 + side} for k in range(1, places)]
    )

    def rows(scorer):
        return pl.ds(pl.multiple_of(scorer * cand, cand), cand)

    def pair_copy(k):
        scorer = lax.rem(place + k, places) * 2 + 1 - side
        return pltpu.make_async_remote_copy(
            src_ref=partial_ref.at[rows(scorer)], dst_ref=pair_ref.at[k],
            send_sem=pair_send.at[k], recv_sem=pair_recv.at[k],
            device_id={"shard": partner}, device_id_type=pl.DeviceIdType.MESH,
        )

    def far_copy(k):
        return pltpu.make_async_remote_copy(
            src_ref=sum_ref.at[k], dst_ref=got_ref.at[k],
            send_sem=far_send.at[k], recv_sem=far_recv.at[k],
            device_id={"shard": lax.rem(place + k, places) * 2 + side},
            device_id_type=pl.DeviceIdType.MESH,
        )

    def fill(scorer):
        queries = select(inverse_ref[rows(scorer), :], unique_ref[...])
        attend(queries, keys_ref, values_ref, scorer, partial_ref, rows(scorer))

    def pair_sum(k):
        pair_copy(k).wait_recv()
        own = partial_ref[rows(lax.rem(place + k, places) * 2 + side), :]
        return own.astype(jnp.float32) + pair_ref[k].astype(jnp.float32)

    @pl.loop(0, places)
    def _(step):
        k = lax.rem(step + 1, places)
        pair = lax.rem(place + k, places) * 2
        fill(pair + 1 - side)
        pair_copy(k).start()
        fill(pair + side)

        @pl.when(step > 0)
        def _():
            sum_ref[step] = pair_sum(step).astype(sum_ref.dtype)
            far_copy(step).start()

    embedded = select(inverse_ref[rows(me), :], table_ref[...])
    gate = project(embedded, w_in_ref[:, :width]).astype(jnp.bfloat16)
    total = pair_sum(0)
    for k in range(1, places):
        far_copy(k).wait_recv()
        total += got_ref[k].astype(jnp.float32)
    gated = layer_norm(total) * gate.astype(jnp.float32)
    out_ref[...] = jnp.dot(
        gated.astype(jnp.bfloat16), w_out_ref[...], preferred_element_type=jnp.float32
    ).astype(out_ref.dtype)

    for k in range(places):
        pair_copy(k).wait_send()
        if k:
            far_copy(k).wait_send()


VMEM = pl.BlockSpec(memory_space=pltpu.VMEM)
SMEM = pl.BlockSpec(memory_space=pltpu.SMEM)


def on_device(cand_table, inverse, cache_keys, cache_values, block_dest, w_in, w_out):
    width = w_out.shape[0]
    cand = inverse.shape[0]
    scorers = lax.axis_size("shard")
    blocks = block_dest.shape[0]
    groups = lax.axis_size("grp")
    dma = pltpu.SemaphoreType.DMA
    table, every_inverse, unique = pl.pallas_call(
        functools.partial(gather_kernel, groups, scorers),
        out_shape=(
            jax.ShapeDtypeStruct((groups, *cand_table.shape), cand_table.dtype),
            jax.ShapeDtypeStruct((scorers, 1, cand), inverse.dtype),
            jax.ShapeDtypeStruct((groups, *cand_table.shape), cand_table.dtype),
        ),
        in_specs=[VMEM] * 3,
        out_specs=(VMEM, VMEM, VMEM),
        scratch_shapes=[
            dma, dma((groups // 2,)), dma((groups // 2,)), dma((groups // 2,)), dma((groups // 2,)),
            dma((scorers,)), dma((scorers,)),
        ],
        compiler_params=pltpu.CompilerParams(
            collective_id=0, has_side_effects=True, vmem_limit_bytes=24 * 2**20
        ),
        name="gather",
    )(cand_table, inverse[None, :], w_in)
    ordered = jax.ShapeDtypeStruct((scorers, MOST * BLK, width), cache_keys.dtype)
    keys, values = pl.pallas_call(
        functools.partial(arrange_kernel, scorers),
        out_shape=(ordered, ordered),
        in_specs=[SMEM, pl.BlockSpec(memory_space=pl.ANY), pl.BlockSpec(memory_space=pl.ANY)],
        out_specs=(VMEM, VMEM),
        scratch_shapes=[pltpu.SMEM((scorers,), jnp.int32), dma((2, blocks))],
        compiler_params=pltpu.CompilerParams(vmem_limit_bytes=24 * 2**20),
        name="arrange",
    )(
        block_dest[:, 0],
        cache_keys.reshape(blocks, BLK, width),
        cache_values.reshape(blocks, BLK, width),
    )
    places = scorers // 2
    buffers = pltpu.VMEM((places, cand, width), jnp.bfloat16)
    return pl.pallas_call(
        functools.partial(reduce_kernel, scorers, cand),
        out_shape=jax.ShapeDtypeStruct((cand, width), jnp.bfloat16),
        in_specs=[VMEM] * 7,
        out_specs=VMEM,
        scratch_shapes=[pltpu.VMEM((scorers * cand, width), jnp.bfloat16)]
        + [buffers] * 3
        + [dma((places,))] * 4,
        compiler_params=pltpu.CompilerParams(
            collective_id=1, has_side_effects=True, vmem_limit_bytes=58 * 2**20
        ),
        name="attend_and_reduce",
    )(
        every_inverse.reshape(-1)[:, None], unique.reshape(-1, width), keys, values,
        table.reshape(-1, width), w_in, w_out,
    )


def solution(mesh):
    rows = P(("grp", "shard"), None)
    in_specs = (P("grp", None), P(("grp", "shard")), rows, rows, rows, P(), P())
    return jax.shard_map(
        on_device, mesh=mesh, in_specs=in_specs, out_specs=rows, check_vma=False
    )
```

time: 78.5 us -> 80.8 us (1.029)
  local copies, waits for them, and re-layouts: 5.06 us -> 12.3 us
  Pallas kernels: 73.2 us -> 68.3 us
    pallas_call x2 -> x1, Pallas kernels: 20.5 us -> 6.79 us  [on_device(): pl.pallas_call(functools.partial(arrange_kernel, scorers), out_shape=(ord...]
    unnamed x11 -> x21, local copies, waits for them, and re-layouts: 1.76 us -> 10.8 us
    pallas_call x1, Pallas kernels: 31.8 us -> 40.5 us  [on_device(): pl.pallas_call(functools.partial(reduce_kernel, scorers, cand), out_shape...]
    slice x1 -> x0, local copies, waits for them, and re-layouts: 2.07 us -> none  [on_device(): w_in[:, :width]]
    another operation x1, local copies, waits for them, and re-layouts: 0.36 us -> 1.44 us  [on_device(): every_inverse.reshape(-1)[:, None]]
    broadcast_in_dim x1 -> x0, local copies, waits for them, and re-layouts: 0.87 us -> none  [on_device(): inverse[:, None]]
where the time goes in v3:
time: 80.8 us; the launch traced here: 80.6 us
  Pallas kernels  68.3 us (85%)
  local copies, waits for them, and re-layouts  12.3 us (15%)
    pallas_call x1, Pallas kernels, on_device(): pl.pallas_call(functools.partial(reduce_kernel, scorers, cand), out_shape...  40.5 us
    pallas_call x1, Pallas kernels, on_device(): pl.pallas_call(functools.partial(gather_kernel, groups, scorers), out_sha...  21.1 us
    unnamed x21, local copies, waits for them, and re-layouts  10.8 us
    pallas_call x1, Pallas kernels, on_device(): pl.pallas_call(functools.partial(arrange_kernel, scorers), out_shape=(ord...  6.79 us

profile of v3, /device:TPU:0, one launch (start us, length us, event | category | flops | bytes accessed | tf_op | source)
XLA Modules:
  0.0 80.6 jit_solution(5425630352068466660)
XLA Ops:
  0.0 0.0 copy-start.1
  0.0 1.6 %copy-done.1 = bf16[2048,512]{1,0:T(8,128)(2,1)S(1)} copy-done((bf16[2048,512]{1,0:T(8,128)(2,1)S(1)}, bf16[2048,512]{1,0:T(8,128)(2,1)}, u32[]{:S(2)}) %copy-start.1) | copy-done | bytes 2097176
  1.6 0.0 copy-start.2
  1.6 1.6 %copy-done.2 = bf16[2048,512]{1,0:T(8,128)(2,1)S(1)} copy-done((bf16[2048,512]{1,0:T(8,128)(2,1)S(1)}, bf16[2048,512]{1,0:T(8,128)(2,1)}, u32[]{:S(2)}) %copy-start.2) | copy-done | bytes 2097176
  3.2 0.0 copy-start.9
  3.2 0.7 copy-done.9
  3.8 0.0 copy-start
  3.8 0.0 copy-start.7
  3.8 0.0 copy-start.8
  3.8 6.8 %arrange.1 = (bf16[8,256,512]{2,1,0:T(8,128)(2,1)S(1)}, bf16[8,256,512]{2,1,0:T(8,128)(2,1)S(1)}) custom-call(s32[16]{0:T(128)S(1)} %bitcast.13, bf16[16,128,512]{2,1,0:T(8,128)(2,1)S(1)} %bitcast.7, bf16[16,128,512]{2,1,0:T(8,128)(2,1)S(1)} %bitcast.8), custom_call_target="tpu_custom_call" | custom-call | tf_op jit(solution)/shard_map/arrange/pallas_call | solution.py:266
  10.6 0.0 copy-start.3
  10.7 1.3 %copy-done.3 = bf16[8,256,512]{2,1,0:T(8,128)(2,1)} copy-done((bf16[8,256,512]{2,1,0:T(8,128)(2,1)}, bf16[8,256,512]{2,1,0:T(8,128)(2,1)S(1)}, u32[]{:S(2)}) %copy-start.3) | copy-done | bytes 2097176
  12.0 0.0 copy-start.4
  12.0 1.3 %copy-done.4 = bf16[8,256,512]{2,1,0:T(8,128)(2,1)} copy-done((bf16[8,256,512]{2,1,0:T(8,128)(2,1)}, bf16[8,256,512]{2,1,0:T(8,128)(2,1)S(1)}, u32[]{:S(2)}) %copy-start.4) | copy-done | bytes 2097176
  13.3 0.0 copy-done
  13.3 0.0 copy-done.7
  13.3 0.0 copy-done.8
  13.3 21.1 %gather.1 = (bf16[4,512,512]{2,1,0:T(8,128)(2,1)S(1)}, s32[8,1,256]{2,1,0:T(1,128)S(1)}, bf16[4,512,512]{2,1,0:T(8,128)(2,1)S(1)}) custom-call(bf16[512,512]{1,0:T(8,128)(2,1)S(1)} %copy-done.7, s32[1,256]{1,0:T(1,128)S(1)} %bitcast.12, bf16[512,1024]{1,0:T(8,128)(2,1)S(1)} %copy-done), custom_call_target="tpu_custom_call" | custom-call | tf_op jit(solution)/shard_map/gather/pallas_call | solution.py:247
  34.4 0.0 copy-start.5
  34.4 1.3 %copy-done.5 = bf16[4,512,512]{2,1,0:T(8,128)(2,1)} copy-done((bf16[4,512,512]{2,1,0:T(8,128)(2,1)}, bf16[4,512,512]{2,1,0:T(8,128)(2,1)S(1)}, u32[]{:S(2)}) %copy-start.5) | copy-done | bytes 2097176
  35.7 0.0 copy-start.6
  35.7 1.3 %copy-done.6 = bf16[4,512,512]{2,1,0:T(8,128)(2,1)} copy-done((bf16[4,512,512]{2,1,0:T(8,128)(2,1)}, bf16[4,512,512]{2,1,0:T(8,128)(2,1)S(1)}, u32[]{:S(2)}) %copy-start.6) | copy-done | bytes 2097176
  37.0 1.4 %copy.8.inverse_ref = s32[2048,1]{1,0:T(8,128)} copy(s32[2048,1]{0,1:T(1,128)S(1)} %bitcast.11) | data formatting | bytes 16384 | tf_op jit(solution)/shard_map/broadcast_in_dim;reshape | solution.py:294
  38.5 40.5 %attend_and_reduce.1 = bf16[256,512]{1,0:T(8,128)(2,1)} custom-call(s32[2048,1]{1,0:T(8,128)} %copy.8.inverse_ref, bf16[2048,512]{1,0:T(8,128)(2,1)} %bitcast.10, bf16[8,256,512]{2,1,0:T(8,128)(2,1)} %copy-done.3, bf16[8,256,512]{2,1,0:T(8,128)(2,1)} %copy-done.4, bf16[2048,512]{1,0:T(8,128)(2,1)} %bitcast.9, bf16[512,1024]{1,0:T(8,128)(2,1)} %w_in_ref.1, ...), custom_call_target="tpu_custom_call" | custom-call | tf_op jit(solution)/shard_map/attend_and_reduce/pallas_call | solution.py:281
  78.9 1.7 %copy.10 = bf16[256,512]{1,0:T(8,128)(2,1)} copy(bf16[256,512]{1,0:T(8,128)(2,1)} %attend_and_reduce.1) | data formatting | bytes 524288
Async XLA Ops:
  0.0 1.6 %copy-start.1 = (bf16[2048,512]{1,0:T(8,128)(2,1)S(1)}, bf16[2048,512]{1,0:T(8,128)(2,1)}, u32[]{:S(2)}) copy-start(bf16[2048,512]{1,0:T(8,128)(2,1)} %param.9) | copy-start | bytes 6291460
  1.6 1.6 %copy-start.2 = (bf16[2048,512]{1,0:T(8,128)(2,1)S(1)}, bf16[2048,512]{1,0:T(8,128)(2,1)}, u32[]{:S(2)}) copy-start(bf16[2048,512]{1,0:T(8,128)(2,1)} %param.10) | copy-start | bytes 6291460
  3.2 0.7 copy-start.9
  3.8 9.5 %copy-start = (bf16[512,1024]{1,0:T(8,128)(2,1)S(1)}, bf16[512,1024]{1,0:T(8,128)(2,1)}, u32[]{:S(2)}) copy-start(bf16[512,1024]{1,0:T(8,128)(2,1)} %w_in_ref.1) | copy-start | bytes 3145732
  3.8 9.5 %copy-start.7 = (bf16[512,512]{1,0:T(8,128)(2,1)S(1)}, bf16[512,512]{1,0:T(8,128)(2,1)}, u32[]{:S(2)}) copy-start(bf16[512,512]{1,0:T(8,128)(2,1)} %own_ref.1) | copy-start | bytes 1572868
  3.8 9.5 %copy-start.8 = (s32[256]{0:T(256)S(1)}, s32[256]{0:T(256)}, u32[]{:S(2)}) copy-start(s32[256]{0:T(256)} %param.8) | copy-start | bytes 3076
  10.6 1.3 %copy-start.3 = (bf16[8,256,512]{2,1,0:T(8,128)(2,1)}, bf16[8,256,512]{2,1,0:T(8,128)(2,1)S(1)}, u32[]{:S(2)}) copy-start(bf16[8,256,512]{2,1,0:T(8,128)(2,1)S(1)} %get-tuple-element.12.keys_ref) | copy-start | bytes 6291460
  12.0 1.3 %copy-start.4 = (bf16[8,256,512]{2,1,0:T(8,128)(2,1)}, bf16[8,256,512]{2,1,0:T(8,128)(2,1)S(1)}, u32[]{:S(2)}) copy-start(bf16[8,256,512]{2,1,0:T(8,128)(2,1)S(1)} %get-tuple-element.13.values_ref) | copy-start | bytes 6291460
  34.4 1.3 %copy-start.5 = (bf16[4,512,512]{2,1,0:T(8,128)(2,1)}, bf16[4,512,512]{2,1,0:T(8,128)(2,1)S(1)}, u32[]{:S(2)}) copy-start(bf16[4,512,512]{2,1,0:T(8,128)(2,1)S(1)} %get-tuple-element.14) | copy-start | bytes 6291460
  35.7 1.3 %copy-start.6 = (bf16[4,512,512]{2,1,0:T(8,128)(2,1)}, bf16[4,512,512]{2,1,0:T(8,128)(2,1)S(1)}, u32[]{:S(2)}) copy-start(bf16[4,512,512]{2,1,0:T(8,128)(2,1)S(1)} %get-tuple-element.11) | copy-start | bytes 6291460

commit v4 on v3

--- a/solution.py
+++ b/solution.py
@@ -269,7 +269,7 @@
         in_specs=[SMEM, pl.BlockSpec(memory_space=pl.ANY), pl.BlockSpec(memory_space=pl.ANY)],
         out_specs=(VMEM, VMEM),
         scratch_shapes=[pltpu.SMEM((scorers,), jnp.int32), dma((2, blocks))],
-        compiler_params=pltpu.CompilerParams(vmem_limit_bytes=24 * 2**20),
+        compiler_params=pltpu.CompilerParams(vmem_limit_bytes=60 * 2**20),
         name="arrange",
     )(
         block_dest[:, 0],

time: 80.8 us -> 73 us (0.903)
  local copies, waits for them, and re-layouts: 12.3 us -> 5.8 us
  Pallas kernels: 68.3 us -> 66.9 us
    unnamed x21 -> x11, local copies, waits for them, and re-layouts: 10.8 us -> 4.37 us
    pallas_call x1, Pallas kernels: 6.79 us -> 5.43 us  [on_device(): pl.pallas_call(functools.partial(arrange_kernel, scorers), out_shape=(ord...]
where the time goes in v4:
time: 73 us; the launch traced here: 72.8 us
  Pallas kernels  66.9 us (92%)
  local copies, waits for them, and re-layouts  5.8 us (8%)
    pallas_call x1, Pallas kernels, on_device(): pl.pallas_call(functools.partial(reduce_kernel, scorers, cand), out_shape...  40.4 us
    pallas_call x1, Pallas kernels, on_device(): pl.pallas_call(functools.partial(gather_kernel, groups, scorers), out_sha...  21.1 us
    pallas_call x1, Pallas kernels, on_device(): pl.pallas_call(functools.partial(arrange_kernel, scorers), out_shape=(ord...  5.43 us
    unnamed x11, local copies, waits for them, and re-layouts  4.37 us

profile of v4, /device:TPU:0, one launch (start us, length us, event | category | flops | bytes accessed | tf_op | source)
XLA Modules:
  0.0 72.8 jit_solution(12587633100380178709)
XLA Ops:
  0.0 0.0 copy-start
  0.0 0.0 copy-start.3
  0.0 0.0 copy-start.4
  0.0 5.4 %arrange.1 = (bf16[8,256,512]{2,1,0:T(8,128)(2,1)}, bf16[8,256,512]{2,1,0:T(8,128)(2,1)}) custom-call(s32[16]{0:T(128)} %bitcast.13, bf16[16,128,512]{2,1,0:T(8,128)(2,1)} %bitcast.11, bf16[16,128,512]{2,1,0:T(8,128)(2,1)} %bitcast.12), custom_call_target="tpu_custom_call" | custom-call | tf_op jit(solution)/shard_map/arrange/pallas_call | solution.py:266
  5.4 0.0 copy-done
  5.5 0.0 copy-done.3
  5.5 0.0 copy-done.4
  5.5 21.1 %gather.1 = (bf16[4,512,512]{2,1,0:T(8,128)(2,1)S(1)}, s32[8,1,256]{2,1,0:T(1,128)S(1)}, bf16[4,512,512]{2,1,0:T(8,128)(2,1)S(1)}) custom-call(bf16[512,512]{1,0:T(8,128)(2,1)S(1)} %copy-done.3, s32[1,256]{1,0:T(1,128)S(1)} %bitcast.10, bf16[512,1024]{1,0:T(8,128)(2,1)S(1)} %copy-done), custom_call_target="tpu_custom_call" | custom-call | tf_op jit(solution)/shard_map/gather/pallas_call | solution.py:247
  26.5 0.0 copy-start.1
  26.6 1.3 %copy-done.1 = bf16[4,512,512]{2,1,0:T(8,128)(2,1)} copy-done((bf16[4,512,512]{2,1,0:T(8,128)(2,1)}, bf16[4,512,512]{2,1,0:T(8,128)(2,1)S(1)}, u32[]{:S(2)}) %copy-start.1) | copy-done | bytes 2097176
  27.9 0.0 copy-start.2
  27.9 1.4 %copy-done.2 = bf16[4,512,512]{2,1,0:T(8,128)(2,1)} copy-done((bf16[4,512,512]{2,1,0:T(8,128)(2,1)}, bf16[4,512,512]{2,1,0:T(8,128)(2,1)S(1)}, u32[]{:S(2)}) %copy-start.2) | copy-done | bytes 2097176
  29.2 1.4 %copy.8.inverse_ref = s32[2048,1]{1,0:T(8,128)} copy(s32[2048,1]{0,1:T(1,128)S(1)} %bitcast.9) | data formatting | bytes 16384 | tf_op jit(solution)/shard_map/broadcast_in_dim;reshape | solution.py:294
  30.7 40.4 %attend_and_reduce.1 = bf16[256,512]{1,0:T(8,128)(2,1)} custom-call(s32[2048,1]{1,0:T(8,128)} %copy.8.inverse_ref, bf16[2048,512]{1,0:T(8,128)(2,1)} %bitcast.8, bf16[8,256,512]{2,1,0:T(8,128)(2,1)} %get-tuple-element.12.keys_ref, bf16[8,256,512]{2,1,0:T(8,128)(2,1)} %get-tuple-element.13.values_ref, bf16[2048,512]{1,0:T(8,128)(2,1)} %bitcast.7, ...), custom_call_target="tpu_custom_call" | custom-call | tf_op jit(solution)/shard_map/attend_and_reduce/pallas_call | solution.py:281
  71.1 1.7 %copy.10 = bf16[256,512]{1,0:T(8,128)(2,1)} copy(bf16[256,512]{1,0:T(8,128)(2,1)} %attend_and_reduce.1) | data formatting | bytes 524288
Async XLA Ops:
  0.0 5.4 %copy-start = (bf16[512,1024]{1,0:T(8,128)(2,1)S(1)}, bf16[512,1024]{1,0:T(8,128)(2,1)}, u32[]{:S(2)}) copy-start(bf16[512,1024]{1,0:T(8,128)(2,1)} %w_in_ref.1) | copy-start | bytes 3145732
  0.0 5.5 %copy-start.3 = (bf16[512,512]{1,0:T(8,128)(2,1)S(1)}, bf16[512,512]{1,0:T(8,128)(2,1)}, u32[]{:S(2)}) copy-start(bf16[512,512]{1,0:T(8,128)(2,1)} %own_ref.1) | copy-start | bytes 1572868
  0.0 5.5 %copy-start.4 = (s32[256]{0:T(256)S(1)}, s32[256]{0:T(256)}, u32[]{:S(2)}) copy-start(s32[256]{0:T(256)} %param.8) | copy-start | bytes 3076
  26.5 1.3 %copy-start.1 = (bf16[4,512,512]{2,1,0:T(8,128)(2,1)}, bf16[4,512,512]{2,1,0:T(8,128)(2,1)S(1)}, u32[]{:S(2)}) copy-start(bf16[4,512,512]{2,1,0:T(8,128)(2,1)S(1)} %get-tuple-element.14) | copy-start | bytes 6291460
  27.9 1.4 %copy-start.2 = (bf16[4,512,512]{2,1,0:T(8,128)(2,1)}, bf16[4,512,512]{2,1,0:T(8,128)(2,1)S(1)}, u32[]{:S(2)}) copy-start(bf16[4,512,512]{2,1,0:T(8,128)(2,1)S(1)} %get-tuple-element.11) | copy-start | bytes 6291460
